TPU v7x, 32 devices: a whole 2x2x4 slice. The times are simulated.
32 devices in a mesh: grp: 4 (over x, core), seq: 8 (over z, y).
Axes of the slice: x: 2, y: 2, z: 4, core: 2. Of those that a mesh axis runs over, the one named last changes fastest.
Arguments:
- tower_input: bfloat16 [65536, 1024], P(('grp', 'seq')), parts along dimension 0, may hold values from -6 to 6
- first_conv_taps: bfloat16 [3, 1024, 512], replicated, may hold values from -0.109375 to 0.109375
- first_conv_bias: float32 [512], replicated, may hold values from -4 to 4
- first_point_weight: bfloat16 [512, 1024], replicated, may hold values from -0.25 to 0.25
- first_point_bias: float32 [1024], replicated, may hold values from -3 to 3
- second_conv_taps: bfloat16 [3, 1024, 512], replicated, may hold values from -0.109375 to 0.109375
- second_conv_bias: float32 [512], replicated, may hold values from -4 to 4
- second_point_weight: bfloat16 [512, 1024], replicated, may hold values from -0.25 to 0.25
- second_point_bias: float32 [1024], replicated, may hold values from -3 to 3
Outputs:
- tower_out: bfloat16 [65536, 1024], P(('grp', 'seq')), parts along dimension 0
There are 4 independent parts, one for each index of `grp`. A program takes and returns all parts, laid end to end along the dimension named above; an argument that names none is the same for every part. Nothing has to cross between parts.
All inputs are finite; a program needn't handle non-finite values.
Results may differ from a plain program's by a relative error of at most 0.01.
Values may be sent and summed in bfloat16 or wider, within the bound.
A program may use at most 128 MiB of HBM per device.

v0:
```python
import jax
import jax.numpy as jnp
from jax import lax
from jax.sharding import PartitionSpec as P


def with_halo(cells, sides, width):
    for axis, dim in sides:
        count = lax.axis_size(axis)
        head = lax.slice_in_dim(cells, 0, width, axis=dim)
        tail = lax.slice_in_dim(cells, cells.shape[dim] - width, cells.shape[dim], axis=dim)
        cells = jnp.concatenate(
            [
                lax.ppermute(tail, axis, [(i, (i + 1) % count) for i in range(count)]),
                cells,
                lax.ppermute(head, axis, [((i + 1) % count, i) for i in range(count)]),
            ],
            axis=dim,
        )
    return cells


def from_behind(value, axis, by):
    size = lax.axis_size(axis)
    return lax.ppermute(value, axis, [(i, (i + by) % size) for i in range(size)])


def activate(values):
    return jax.nn.gelu(values.astype(jnp.float32)).astype(jnp.bfloat16)


def rounded_product(acts, tap):
    return jnp.dot(acts, tap, preferred_element_type=jnp.float32).astype(jnp.bfloat16)


def widen(product):
    return lax.optimization_barrier(product).astype(jnp.float32)


def finish(block_in, total, bias_conv, point, bias_point):
    middle = jax.nn.gelu(total + bias_conv).astype(jnp.bfloat16)
    branch = jnp.dot(middle, point, preferred_element_type=jnp.float32)
    return (block_in.astype(jnp.float32) + branch + bias_point).astype(jnp.bfloat16)


def near_layer(block_in, rimmed, taps, bias_conv, point, bias_point):
    rows = block_in.shape[0]
    spacing = (rimmed.shape[0] - rows) // 2
    total = jnp.dot(rimmed[spacing : spacing + rows], taps[1], preferred_element_type=jnp.float32)
    total = total + jnp.dot(rimmed[0:rows], taps[0], preferred_element_type=jnp.float32)
    total = total + jnp.dot(
        rimmed[2 * spacing : 2 * spacing + rows], taps[2], preferred_element_type=jnp.float32
    )
    return finish(block_in, total, bias_conv, point, bias_point)


def per_device(
    tower_input,
    first_conv_taps,
    first_conv_bias,
    first_point_weight,
    first_point_bias,
    second_conv_taps,
    second_conv_bias,
    second_point_weight,
    second_point_bias,
):
    rows = tower_input.shape[0]
    spacing = rows // 4
    acts_near = activate(tower_input)
    rimmed = with_halo(acts_near, (("seq", 0),), spacing)
    single_residual_layer = near_layer(
        tower_input, rimmed, first_conv_taps, first_conv_bias, first_point_weight, first_point_bias
    )
    acts_far = activate(single_residual_layer)
    back_acts = from_behind(acts_far, "seq", 2)
    ahead_acts = from_behind(acts_far, "seq", -2)
    total = jnp.dot(acts_far, second_conv_taps[1], preferred_element_type=jnp.float32)
    total = total + widen(rounded_product(back_acts, second_conv_taps[0]))
    total = total + widen(rounded_product(ahead_acts, second_conv_taps[2]))
    return finish(
        single_residual_layer, total, second_conv_bias, second_point_weight, second_point_bias
    )


def solution(mesh):
    return jax.shard_map(
        per_device,
        mesh=mesh,
        in_specs=(P(("grp", "seq"), None), P(), P(), P(), P(), P(), P(), P(), P()),
        out_specs=P(("grp", "seq"), None),
        check_vma=False,
    )
```

profile of v0, /device:TPU:0, one launch (start us, length us, event | category | flops | bytes accessed | tf_op | source)
XLA Modules:
  0.0 271.7 jit_solution(2828211144233290418)
XLA Ops:
  0.0 0.0 copy-start
  0.0 0.0 copy-start.3
  0.0 4.6 %fusion.5 = bf16[2048,1024]{1,0:T(8,128)(2,1)S(1)} fusion(bf16[2048,1024]{1,0:T(8,128)(2,1)} %param.9), kind=kLoop, calls=%fused_computation.15 | loop fusion | flops 20971520 | bytes 8388608 | tf_op jit(solution)/shard_map/convert_element_type | solution.py:29
  4.6 0.0 copy-start.1
  4.6 0.0 copy-start.2
  4.7 0.2 fusion.78
  4.8 3.0 %collective-permute-start = (bf16[512,1024]{1,0:T(8,128)(2,1)S(1)}, bf16[512,1024]{1,0:T(8,128)(2,1)S(1)}, u32[]{:S(2)}, u32[]{:S(2)}) collective-permute-start(bf16[512,1024]{1,0:T(8,128)(2,1)S(1)} %get-tuple-element.6), channel_id=1, source_target_pairs={{0,1},{1,2},{2,3},{3,4},{4,5},{5,6},{6,7},{7,0},{8,9},{9,10},{10,1... | collective-permute-start | bytes 3145736 | tf_op jit(solution)/shard_map/ppermute | solution.py:14
  7.9 3.1 %collective-permute-start.1 = (bf16[512,1024]{1,0:T(8,128)(2,1)S(1)}, bf16[512,1024]{1,0:T(8,128)(2,1)S(1)}, u32[]{:S(2)}, u32[]{:S(2)}) collective-permute-start(bf16[512,1024]{1,0:T(8,128)(2,1)S(1)} %get-tuple-element.5), channel_id=1, source_target_pairs={{1,0},{2,1},{3,2},{4,3},{5,4},{6,5},{7,6},{0,7},{9,8},{10,9},{11,1... | collective-permute-start | bytes 3145736 | tf_op jit(solution)/shard_map/ppermute | solution.py:16
  11.0 0.0 copy-done.3
  11.0 0.0 copy-done.2
  11.0 4.6 %fusion.54 = f32[2048,512]{1,0:T(8,128)} fusion(bf16[3,1024,512]{2,1,0:T(8,128)(2,1)S(1)} %copy-done.3, bf16[2048,1024]{1,0:T(8,128)(2,1)S(1)} %copy-done.2), kind=kOutput, calls=%fused_computation.63 | convolution fusion | flops 2168455168 | bytes 9437184 | tf_op jit(solution)/shard_map/dot_general | solution.py:49
  15.5 0.0 copy-start.5
  15.5 0.0 copy-start.7
  15.5 37.2 %collective-permute-done = bf16[512,1024]{1,0:T(8,128)(2,1)S(1)} collective-permute-done((bf16[512,1024]{1,0:T(8,128)(2,1)S(1)}, bf16[512,1024]{1,0:T(8,128)(2,1)S(1)}, u32[]{:S(2)}, u32[]{:S(2)}) %collective-permute-start) | collective-permute-done | bytes 1048608 | tf_op jit(solution)/shard_map/ppermute | solution.py:14
  52.7 0.0 copy-done.1
  52.7 4.4 %fusion.34 = f32[2048,512]{1,0:T(8,128)} fusion(bf16[2048,1024]{1,0:T(8,128)(2,1)S(1)} %fusion.5, bf16[512,1024]{1,0:T(8,128)(2,1)S(1)} %collective-permute-done, bf16[3,1024,512]{2,1,0:T(8,128)(2,1)S(1)} %copy-done.3), kind=kOutput, calls=%fused_computation.48 | convolution fusion | flops 2155872256 | bytes 10485760 | tf_op jit(solution)/shard_map/dot_general | solution.py:50
  57.1 0.0 collective-permute-done.1
  57.1 0.0 copy-done
  57.1 0.0 copy-done.5
  57.1 0.0 copy-done.7
  57.1 14.4 %fusion.13 = (bf16[2048,1024]{1,0:T(8,128)(2,1)}, bf16[2048,1024]{1,0:T(8,128)(2,1)}) fusion(f32[1024]{0:T(1024)S(1)} %copy-done.5, bf16[512,1024]{1,0:T(8,128)(2,1)S(1)} %copy-done, f32[2048,512]{1,0:T(8,128)} %fusion.54, f32[2048,512]{1,0:T(8,128)} %fusion.34, bf16[512,1024]{1,0:T(8,128)(2,1)S(1)} %collective-permute-done.1, ...), kind=kOutput, calls=%fused_computation.23 | convolution fusion | flops 4345298944 | bytes 28317696 | tf_op jit(solution)/shard_map/dot_general | solution.py:42
  71.5 1.6 collective-permute-start.2
  73.1 2.3 collective-permute-start.3
  75.4 91.7 %collective-permute-done.2 = bf16[2048,1024]{1,0:T(8,128)(2,1)S(1)} collective-permute-done((bf16[2048,1024]{1,0:T(8,128)(2,1)}, bf16[2048,1024]{1,0:T(8,128)(2,1)S(1)}, u32[]{:S(2)}, u32[]{:S(2)}) %collective-permute-start.2) | collective-permute-done | bytes 4194336 | tf_op jit(solution)/shard_map/ppermute | solution.py:25
  167.1 5.0 %convolution_convert_fusion.1 = bf16[2048,512]{1,0:T(8,128)(2,1)} fusion(bf16[2048,1024]{1,0:T(8,128)(2,1)S(1)} %collective-permute-done.2, bf16[3,1024,512]{2,1,0:T(8,128)(2,1)} %param.14), kind=kOutput, calls=%fused_computation.51 | convolution fusion | flops 2148532224 | bytes 7340032 | tf_op jit(solution)/shard_map/dot_general | solution.py:33
  172.1 0.0 copy-start.4
  172.1 0.0 copy-start.6
  172.1 0.0 copy-start.8
  172.1 82.3 %collective-permute-done.3 = bf16[2048,1024]{1,0:T(8,128)(2,1)S(1)} collective-permute-done((bf16[2048,1024]{1,0:T(8,128)(2,1)}, bf16[2048,1024]{1,0:T(8,128)(2,1)S(1)}, u32[]{:S(2)}, u32[]{:S(2)}) %collective-permute-start.3) | collective-permute-done | bytes 4194336 | tf_op jit(solution)/shard_map/ppermute | solution.py:25
  254.4 4.9 %convolution_convert_fusion = bf16[2048,512]{1,0:T(8,128)(2,1)} fusion(bf16[2048,1024]{1,0:T(8,128)(2,1)S(1)} %collective-permute-done.3, bf16[3,1024,512]{2,1,0:T(8,128)(2,1)} %param.14), kind=kOutput, calls=%fused_computation.50 | convolution fusion | flops 2148532224 | bytes 7340032 | tf_op jit(solution)/shard_map/dot_general | solution.py:33
  259.3 0.0 copy-done.4
  259.3 0.0 copy-done.6
  259.3 0.0 copy-done.8
  259.3 12.4 %fusion.15 = bf16[2048,1024]{1,0:T(8,128)(2,1)} fusion(bf16[2048,1024]{1,0:T(8,128)(2,1)} %get-tuple-element.8, f32[1024]{0:T(1024)S(1)} %copy-done.6, bf16[512,1024]{1,0:T(8,128)(2,1)S(1)} %copy-done.4, bf16[2048,512]{1,0:T(8,128)(2,1)} %convolution_convert_fusion, bf16[2048,512]{1,0:T(8,128)(2,1)} %convolution_convert_fusion.1, f32[512]{0:T(512)S(1)} %copy-done.8, ...), kind=kOutput, calls=%fused_computation.25 | convolution fusion | flops 4339007488 | bytes 18880512 | tf_op jit(solution)/shard_map/dot_general | solution.py:42
Async XLA Ops:
  0.0 57.1 %copy-start = (bf16[512,1024]{1,0:T(8,128)(2,1)S(1)}, bf16[512,1024]{1,0:T(8,128)(2,1)}, u32[]{:S(2)}) copy-start(bf16[512,1024]{1,0:T(8,128)(2,1)} %param.12) | copy-start | bytes 3145732
  0.0 11.0 %copy-start.3 = (bf16[3,1024,512]{2,1,0:T(8,128)(2,1)S(1)}, bf16[3,1024,512]{2,1,0:T(8,128)(2,1)}, u32[]{:S(2)}) copy-start(bf16[3,1024,512]{2,1,0:T(8,128)(2,1)} %param.10) | copy-start | bytes 9437188
  4.6 48.1 %copy-start.1 = (bf16[2048,1024]{1,0:T(8,128)(2,1)}, bf16[2048,1024]{1,0:T(8,128)(2,1)S(1)}, u32[]{:S(2)}) copy-start(bf16[2048,1024]{1,0:T(8,128)(2,1)S(1)} %fusion.5) | copy-start | bytes 12582916
  4.6 6.3 %copy-start.2 = (bf16[2048,1024]{1,0:T(8,128)(2,1)S(1)}, bf16[2048,1024]{1,0:T(8,128)(2,1)}, u32[]{:S(2)}) copy-start(bf16[2048,1024]{1,0:T(8,128)(2,1)} %param.9) | copy-start | bytes 12582916
  4.8 47.9 %collective-permute-start = (bf16[512,1024]{1,0:T(8,128)(2,1)S(1)}, bf16[512,1024]{1,0:T(8,128)(2,1)S(1)}, u32[]{:S(2)}, u32[]{:S(2)}) collective-permute-start(bf16[512,1024]{1,0:T(8,128)(2,1)S(1)} %get-tuple-element.6), channel_id=1, source_target_pairs={{0,1},{1,2},{2,3},{3,4},{4,5},{5,6},{6,7},{7,0},{8,9},{9,10},{10,1... | collective-permute-start | bytes 3145736 | tf_op jit(solution)/shard_map/ppermute | solution.py:14
  7.9 49.3 %collective-permute-start.1 = (bf16[512,1024]{1,0:T(8,128)(2,1)S(1)}, bf16[512,1024]{1,0:T(8,128)(2,1)S(1)}, u32[]{:S(2)}, u32[]{:S(2)}) collective-permute-start(bf16[512,1024]{1,0:T(8,128)(2,1)S(1)} %get-tuple-element.5), channel_id=1, source_target_pairs={{1,0},{2,1},{3,2},{4,3},{5,4},{6,5},{7,6},{0,7},{9,8},{10,9},{11,1... | collective-permute-start | bytes 3145736 | tf_op jit(solution)/shard_map/ppermute | solution.py:16
  15.5 41.6 %copy-start.5 = (f32[1024]{0:T(1024)S(1)}, f32[1024]{0:T(1024)}, u32[]{:S(2)}) copy-start(f32[1024]{0:T(1024)} %param.13) | copy-start | bytes 12292
  15.5 41.6 %copy-start.7 = (f32[512]{0:T(512)S(1)}, f32[512]{0:T(512)}, u32[]{:S(2)}) copy-start(f32[512]{0:T(512)} %param.11) | copy-start | bytes 6148
  71.5 95.6 %collective-permute-start.2 = (bf16[2048,1024]{1,0:T(8,128)(2,1)}, bf16[2048,1024]{1,0:T(8,128)(2,1)S(1)}, u32[]{:S(2)}, u32[]{:S(2)}) collective-permute-start(bf16[2048,1024]{1,0:T(8,128)(2,1)} %get-tuple-element.7), channel_id=1, source_target_pairs={{0,2},{1,3},{2,4},{3,5},{4,6},{5,7},{6,0},{7,1},{8,10},{9,11},{10,... | collective-permute-start | bytes 12582920 | tf_op jit(solution)/shard_map/ppermute | solution.py:25
  73.1 181.3 %collective-permute-start.3 = (bf16[2048,1024]{1,0:T(8,128)(2,1)}, bf16[2048,1024]{1,0:T(8,128)(2,1)S(1)}, u32[]{:S(2)}, u32[]{:S(2)}) collective-permute-start(bf16[2048,1024]{1,0:T(8,128)(2,1)} %get-tuple-element.7), channel_id=1, source_target_pairs={{0,6},{1,7},{2,0},{3,1},{4,2},{5,3},{6,4},{7,5},{8,14},{9,15},{10,... | collective-permute-start | bytes 12582920 | tf_op jit(solution)/shard_map/ppermute | solution.py:25
  172.1 87.2 %copy-start.4 = (bf16[512,1024]{1,0:T(8,128)(2,1)S(1)}, bf16[512,1024]{1,0:T(8,128)(2,1)}, u32[]{:S(2)}) copy-start(bf16[512,1024]{1,0:T(8,128)(2,1)} %param.16) | copy-start | bytes 3145732
  172.1 87.2 %copy-start.6 = (f32[1024]{0:T(1024)S(1)}, f32[1024]{0:T(1024)}, u32[]{:S(2)}) copy-start(f32[1024]{0:T(1024)} %param.17) | copy-start | bytes 12292
  172.1 87.2 %copy-start.8 = (f32[512]{0:T(512)S(1)}, f32[512]{0:T(512)}, u32[]{:S(2)}) copy-start(f32[512]{0:T(512)} %param.15) | copy-start | bytes 6148
where the time goes:
time: 275 us; the launch traced here: 272 us
  waiting for transfers between devices  211 us (77%)
  matrix products  45.6 us (17%)
  starting transfers between devices  9.96 us (4%)
  other arithmetic  4.62 us (2%)
    ppermute x2, waiting for transfers between devices, from_behind(): lax.ppermute(value, axis, [(i, (i + by) % size) for i in range(size)])  174 us
    ppermute x1, waiting for transfers between devices, with_halo(): lax.ppermute(tail, axis, [(i, (i + 1) % count) for i in range(count)])  37.2 us
    dot_general x2, matrix products, finish(): branch = jnp.dot(middle, point, preferred_element_type=jnp.float32)  26.8 us
    dot_general x2, matrix products, rounded_product(): jnp.dot(acts, tap, preferred_element_type=jnp.float32).astype(jnp.bfloat16)  9.92 us
  transfers between devices with their start and end apart: 4, of which 3 were waited for; matrix products, arithmetic and copies ran while one was open for 5% of the time, Pallas kernels for 0%

commit v1 on v0

v1 whole, which is shorter than its diff:
```python
import jax
import jax.numpy as jnp
from jax import lax
from jax.sharding import PartitionSpec as P


def shifted(value, axis, by):
    size = lax.axis_size(axis)
    return lax.ppermute(value, axis, [(i, (i + by) % size) for i in range(size)])


def activate(values):
    return jax.nn.gelu(values.astype(jnp.float32)).astype(jnp.bfloat16)


def product(acts, tap):
    return jnp.dot(acts, tap, preferred_element_type=jnp.float32)


def rounded_product(acts, tap):
    return product(acts, tap).astype(jnp.bfloat16)


def finish(block_in, total, bias_conv, point, bias_point):
    middle = jax.nn.gelu(total + bias_conv).astype(jnp.bfloat16)
    branch = jnp.dot(middle, point, preferred_element_type=jnp.float32)
    return (block_in.astype(jnp.float32) + branch + bias_point).astype(jnp.bfloat16)


def per_device(
    tower_input,
    first_conv_taps,
    first_conv_bias,
    first_point_weight,
    first_point_bias,
    second_conv_taps,
    second_conv_bias,
    second_point_weight,
    second_point_bias,
):
    rows = tower_input.shape[0]
    d = rows // 4
    t0, t1, t2 = first_conv_taps[0], first_conv_taps[1], first_conv_taps[2]
    near = (first_conv_bias, first_point_weight, first_point_bias)
    far = (second_conv_bias, second_point_weight, second_point_bias)
    xs = [tower_input[i * d : (i + 1) * d] for i in range(4)]
    a = [activate(x) for x in xs]
    from_prev = shifted(rounded_product(a[3], t0), "seq", 1)
    from_next = shifted(rounded_product(a[0], t2), "seq", -1)

    def far_products(layer):
        acts = activate(layer)
        behind = shifted(rounded_product(acts, second_conv_taps[0]), "seq", 2)
        ahead = shifted(rounded_product(acts, second_conv_taps[2]), "seq", -2)
        return acts, behind, ahead

    def inner(i):
        total = product(a[i - 1], t0) + product(a[i], t1) + product(a[i + 1], t2)
        return finish(xs[i], total, *near)

    layers = [None] * 4
    parts = [None] * 4
    for i in (1, 2):
        layers[i] = inner(i)
        parts[i] = far_products(layers[i])
    total = product(a[0], t1) + product(a[1], t2) + from_prev.astype(jnp.float32)
    layers[0] = finish(xs[0], total, *near)
    parts[0] = far_products(layers[0])
    total = product(a[3], t1) + product(a[2], t0) + from_next.astype(jnp.float32)
    layers[3] = finish(xs[3], total, *near)
    parts[3] = far_products(layers[3])
    outs = []
    for i in range(4):
        acts, behind, ahead = parts[i]
        total = product(acts, second_conv_taps[1])
        total = total + behind.astype(jnp.float32) + ahead.astype(jnp.float32)
        outs.append(finish(layers[i], total, *far))
    return jnp.concatenate(outs, axis=0)


def solution(mesh):
    return jax.shard_map(
        per_device,
        mesh=mesh,
        in_specs=(P(("grp", "seq"), None), P(), P(), P(), P(), P(), P(), P(), P()),
        out_specs=P(("grp", "seq"), None),
        check_vma=False,
    )
```

time: 275 us -> 124 us (0.45); the launches traced: 272 us -> 124 us
  waiting for transfers between devices: 211 us -> 21.7 us
  matrix products: 45.6 us -> 75.4 us
  starting transfers between devices: 9.96 us -> 22.1 us
    ppermute x4 -> x10, waiting for transfers between devices: 211 us -> 21.7 us  [shifted(): lax.ppermute(value, axis, [(i, (i + by) % size) for i in range(size)])]
    dot_general x4 -> x16, matrix products: 18.9 us -> 37.7 us  [product(): return jnp.dot(acts, tap, preferred_element_type=jnp.float32)]
    ppermute x4 -> x10, starting transfers between devices: 9.96 us -> 22.1 us  [shifted(): lax.ppermute(value, axis, [(i, (i + by) % size) for i in range(size)])]
    dot_general x2 -> x8, matrix products: 26.8 us -> 37.7 us  [finish(): branch = jnp.dot(middle, point, preferred_element_type=jnp.float32)]
    convert_element_type x1 -> x0, other arithmetic: 4.62 us -> none  [activate(): return jax.nn.gelu(values.astype(jnp.float32)).astype(jnp.bfloat16)]
    concatenate x0 -> x1, other arithmetic: none -> 3.4 us  [per_device(): return jnp.concatenate(outs, axis=0)]
  transfers between devices with their start and end apart: 4 -> 10, of which waited for: 3 -> 3; matrix products, arithmetic and copies ran while one was open for 5% -> 55% of each run, Pallas kernels for 0% -> 0%
where the time goes in v1:
time: 124 us
  matrix products  75.4 us (61%)
  starting transfers between devices  22.1 us (18%)
  waiting for transfers between devices  21.7 us (18%)
  other arithmetic  3.4 us (3%)
  local copies, waits for them, and re-layouts  1.45 us (1%)
    dot_general x8, matrix products, finish(): branch = jnp.dot(middle, point, preferred_element_type=jnp.float32)  37.7 us
    dot_general x16, matrix products, product(): return jnp.dot(acts, tap, preferred_element_type=jnp.float32)  37.7 us
    ppermute x10, starting transfers between devices, shifted(): lax.ppermute(value, axis, [(i, (i + by) % size) for i in range(size)])  22.1 us
    ppermute x10, waiting for transfers between devices, shifted(): lax.ppermute(value, axis, [(i, (i + by) % size) for i in range(size)])  21.7 us
    concatenate x1, other arithmetic, per_device(): return jnp.concatenate(outs, axis=0)  3.4 us
  transfers between devices with their start and end apart: 10, of which 3 were waited for; matrix products, arithmetic and copies ran while one was open for 55% of the time, Pallas kernels for 0%

profile of v1, /device:TPU:0, one launch (start us, length us, event | category | flops | bytes accessed | tf_op | source)
XLA Modules:
  0.0 124.2 jit_solution(16356965175267191333)
XLA Ops:
  0.0 0.0 copy-start
  0.0 2.6 %convolution_convert_fusion.9 = bf16[512,512]{1,0:T(8,128)(2,1)S(1)} fusion(bf16[3,1024,512]{2,1,0:T(8,128)(2,1)} %param.10, bf16[2048,1024]{1,0:T(8,128)(2,1)} %param.9), kind=kOutput, calls=%fused_computation.130 | convolution fusion | flops 542375936 | bytes 2621440 | tf_op jit(solution)/shard_map/dot_general | solution.py:17
  2.6 3.0 %collective-permute-start = (bf16[512,512]{1,0:T(8,128)(2,1)S(1)}, bf16[512,512]{1,0:T(8,128)(2,1)S(1)}, u32[]{:S(2)}, u32[]{:S(2)}) collective-permute-start(bf16[512,512]{1,0:T(8,128)(2,1)S(1)} %convolution_convert_fusion.9), channel_id=1, source_target_pairs={{0,1},{1,2},{2,3},{3,4},{4,5},{5,6},{6,7},{7,0},{8,9},{9,10},{10,1... | collective-permute-start | bytes 1572872 | tf_op jit(solution)/shard_map/ppermute | solution.py:9
  5.6 0.0 copy-done.4
  5.6 0.0 copy-done.1
  5.6 1.7 %convolution_convert_fusion.2 = bf16[512,512]{1,0:T(8,128)(2,1)} fusion(bf16[3,1024,512]{2,1,0:T(8,128)(2,1)S(1)} %copy-done.4, bf16[2048,1024]{1,0:T(8,128)(2,1)S(1)} %copy-done.1), kind=kOutput, calls=%fused_computation.123 | convolution fusion | flops 542375936 | bytes 2621440 | tf_op jit(solution)/shard_map/dot_general | solution.py:17
  7.3 4.2 %collective-permute-start.7 = (bf16[512,512]{1,0:T(8,128)(2,1)}, bf16[512,512]{1,0:T(8,128)(2,1)}, u32[]{:S(2)}, u32[]{:S(2)}) collective-permute-start(bf16[512,512]{1,0:T(8,128)(2,1)} %convolution_convert_fusion.2), channel_id=1, source_target_pairs={{0,7},{1,0},{2,1},{3,2},{4,3},{5,4},{6,5},{7,6},{8,15},{9,8},{10,9... | collective-permute-start | bytes 1572872 | tf_op jit(solution)/shard_map/ppermute | solution.py:9
  11.5 0.9 fusion.149
  12.4 0.0 copy-start.10
  12.4 0.0 copy-start.12
  12.4 0.9 convolution_add_fusion.4
  13.3 0.0 copy-done
  13.3 0.0 copy-done.10
  13.3 0.0 copy-done.12
  13.3 4.5 %fusion.15 = bf16[512,1024]{1,0:T(8,128)(2,1)} fusion(bf16[512,1024]{1,0:T(8,128)(2,1)S(1)} %copy-done, f32[1024]{0:T(1024)S(1)} %copy-done.10, bf16[2048,1024]{1,0:T(8,128)(2,1)} %param.9, f32[512,512]{1,0:T(8,128)S(1)} %convolution_add_fusion.4, bf16[3,1024,512]{2,1,0:T(8,128)(2,1)} %param.10, f32[512]{0:T(512)S(1)} %copy-done.12), kind=kOutput, calls=%fused_computation.56 | convolution fusion | flops 1083965440 | bytes 6297600 | tf_op jit(solution)/shard_map/dot_general | solution.py:26
  17.9 3.4 %convolution_convert_fusion.6 = bf16[512,512]{1,0:T(8,128)(2,1)} fusion(bf16[3,1024,512]{2,1,0:T(8,128)(2,1)} %param.14, bf16[512,1024]{1,0:T(8,128)(2,1)} %fusion.15), kind=kOutput, calls=%fused_computation.127 | convolution fusion | flops 542375936 | bytes 2621440 | tf_op jit(solution)/shard_map/dot_general | solution.py:17
  21.3 0.0 collective-permute-start.3
  21.3 0.0 copy-done.15
  21.3 3.1 %convolution_convert_fusion.5 = bf16[512,512]{1,0:T(8,128)(2,1)} fusion(bf16[3,1024,512]{2,1,0:T(8,128)(2,1)} %param.14, bf16[512,1024]{1,0:T(8,128)(2,1)S(1)} %copy-done.15), kind=kOutput, calls=%fused_computation.126 | convolution fusion | flops 542375936 | bytes 2621440 | tf_op jit(solution)/shard_map/dot_general | solution.py:17
  24.4 3.7 %collective-permute-start.4 = (bf16[512,512]{1,0:T(8,128)(2,1)}, bf16[512,512]{1,0:T(8,128)(2,1)S(1)}, u32[]{:S(2)}, u32[]{:S(2)}) collective-permute-start(bf16[512,512]{1,0:T(8,128)(2,1)} %convolution_convert_fusion.5), channel_id=1, source_target_pairs={{0,6},{1,7},{2,0},{3,1},{4,2},{5,3},{6,4},{7,5},{8,14},{9,15},{10,... | collective-permute-start | bytes 1572872 | tf_op jit(solution)/shard_map/ppermute | solution.py:9
  28.0 0.0 copy-done.2
  28.0 0.0 copy-done.5
  28.1 0.9 fusion.147
  28.9 1.9 %convolution_add_fusion.2 = f32[512,512]{1,0:T(8,128)} fusion(f32[512,512]{1,0:T(8,128)S(1)} %fusion.147, bf16[3,1024,512]{2,1,0:T(8,128)(2,1)S(1)} %copy-done.5, bf16[2048,1024]{1,0:T(8,128)(2,1)S(1)} %copy-done.2), kind=kOutput, calls=%fused_computation.116 | convolution fusion | flops 542375936 | bytes 4194304 | tf_op jit(solution)/shard_map/dot_general | solution.py:17
  30.8 4.8 %fusion.39 = bf16[512,1024]{1,0:T(8,128)(2,1)} fusion(bf16[512,1024]{1,0:T(8,128)(2,1)S(1)} %copy-done, f32[1024]{0:T(1024)S(1)} %copy-done.10, bf16[2048,1024]{1,0:T(8,128)(2,1)} %param.9, f32[512,512]{1,0:T(8,128)} %convolution_add_fusion.2, bf16[3,1024,512]{2,1,0:T(8,128)(2,1)} %param.10, f32[512]{0:T(512)S(1)} %copy-done.12), kind=kOutput, calls=%fused_computation.80 | convolution fusion | flops 1083965440 | bytes 6297600 | tf_op jit(solution)/shard_map/dot_general | solution.py:26
  35.6 3.4 %convolution_convert_fusion.4 = bf16[512,512]{1,0:T(8,128)(2,1)} fusion(bf16[3,1024,512]{2,1,0:T(8,128)(2,1)} %param.14, bf16[512,1024]{1,0:T(8,128)(2,1)} %fusion.39), kind=kOutput, calls=%fused_computation.125 | convolution fusion | flops 542375936 | bytes 2621440 | tf_op jit(solution)/shard_map/dot_general | solution.py:17
  39.0 0.0 collective-permute-start.5
  39.0 0.0 copy-done.3
  39.0 0.6 copy-done.6
  39.6 1.8 %fusion.156 = f32[512,512]{1,0:T(8,128)} fusion(bf16[3,1024,512]{2,1,0:T(8,128)(2,1)S(1)} %copy-done.6, bf16[2048,1024]{1,0:T(8,128)(2,1)S(1)} %copy-done.3), kind=kOutput, calls=%fused_computation.221 | convolution fusion | flops 542113792 | bytes 3145728 | tf_op jit(solution)/shard_map/dot_general | solution.py:17
  41.4 0.0 copy-done.14
  41.4 2.9 %convolution_convert_fusion.3 = bf16[512,512]{1,0:T(8,128)(2,1)} fusion(bf16[3,1024,512]{2,1,0:T(8,128)(2,1)} %param.14, bf16[512,1024]{1,0:T(8,128)(2,1)S(1)} %copy-done.14), kind=kOutput, calls=%fused_computation.124 | convolution fusion | flops 542375936 | bytes 2621440 | tf_op jit(solution)/shard_map/dot_general | solution.py:17
  44.4 1.8 %fusion.160 = f32[512,512]{1,0:T(8,128)} fusion(bf16[3,1024,512]{2,1,0:T(8,128)(2,1)S(1)} %copy-done.6, bf16[2048,1024]{1,0:T(8,128)(2,1)S(1)} %copy-done.3), kind=kOutput, calls=%fused_computation.225 | convolution fusion | flops 542113792 | bytes 3145728 | tf_op jit(solution)/shard_map/dot_general | solution.py:17
  46.2 0.0 collective-permute-done.7
  46.2 3.2 %collective-permute-start.6 = (bf16[512,512]{1,0:T(8,128)(2,1)}, bf16[512,512]{1,0:T(8,128)(2,1)}, u32[]{:S(2)}, u32[]{:S(2)}) collective-permute-start(bf16[512,512]{1,0:T(8,128)(2,1)} %convolution_convert_fusion.3), channel_id=1, source_target_pairs={{0,6},{1,7},{2,0},{3,1},{4,2},{5,3},{6,4},{7,5},{8,14},{9,15},{10,... | collective-permute-start | bytes 1572872 | tf_op jit(solution)/shard_map/ppermute | solution.py:9
  49.4 5.0 %fusion.23 = bf16[512,1024]{1,0:T(8,128)(2,1)} fusion(bf16[512,1024]{1,0:T(8,128)(2,1)S(1)} %copy-done, f32[1024]{0:T(1024)S(1)} %copy-done.10, bf16[2048,1024]{1,0:T(8,128)(2,1)} %param.9, bf16[512,512]{1,0:T(8,128)(2,1)} %collective-permute-done.7, f32[512,512]{1,0:T(8,128)} %fusion.156, bf16[3,1024,512]{2,1,0:T(8,128)(2,1)} %param.10, f32[512]{0:T(512)S(1)} %copy-done.12), kind=kOutput, calls=%fused_computation.64 | convolution fusion | flops 1084489728 | bytes 6821888 | tf_op jit(solution)/shard_map/dot_general | solution.py:26
  54.4 3.3 %convolution_convert_fusion = bf16[512,512]{1,0:T(8,128)(2,1)} fusion(bf16[3,1024,512]{2,1,0:T(8,128)(2,1)} %param.14, bf16[512,1024]{1,0:T(8,128)(2,1)} %fusion.23), kind=kOutput, calls=%fused_computation.121 | convolution fusion | flops 542375936 | bytes 2621440 | tf_op jit(solution)/shard_map/dot_general | solution.py:17
  57.7 0.0 copy-done.16
  57.7 2.9 %convolution_convert_fusion.1 = bf16[512,512]{1,0:T(8,128)(2,1)} fusion(bf16[3,1024,512]{2,1,0:T(8,128)(2,1)} %param.14, bf16[512,1024]{1,0:T(8,128)(2,1)S(1)} %copy-done.16), kind=kOutput, calls=%fused_computation.122 | convolution fusion | flops 542375936 | bytes 2621440 | tf_op jit(solution)/shard_map/dot_general | solution.py:17
  60.6 0.0 collective-permute-done
  60.6 0.0 collective-permute-start.8
  60.6 4.9 %fusion.7 = bf16[512,1024]{1,0:T(8,128)(2,1)} fusion(bf16[512,1024]{1,0:T(8,128)(2,1)S(1)} %copy-done, f32[1024]{0:T(1024)S(1)} %copy-done.10, bf16[2048,1024]{1,0:T(8,128)(2,1)} %param.9, bf16[512,512]{1,0:T(8,128)(2,1)S(1)} %collective-permute-done, f32[512,512]{1,0:T(8,128)} %fusion.160, bf16[3,1024,512]{2,1,0:T(8,128)(2,1)} %param.10, f32[512]{0:T(512)S(1)} %copy-done.12), kind=kOutput, calls=%fused_computation.48 | convolution fusion | flops 1084489728 | bytes 6821888 | tf_op jit(solution)/shard_map/dot_general | solution.py:26
  65.5 3.3 %convolution_convert_fusion.7 = bf16[512,512]{1,0:T(8,128)(2,1)} fusion(bf16[3,1024,512]{2,1,0:T(8,128)(2,1)} %param.14, bf16[512,1024]{1,0:T(8,128)(2,1)} %fusion.7), kind=kOutput, calls=%fused_computation.128 | convolution fusion | flops 542375936 | bytes 2621440 | tf_op jit(solution)/shard_map/dot_general | solution.py:17
  68.8 0.0 copy-done.17
  68.8 3.0 %convolution_convert_fusion.8 = bf16[512,512]{1,0:T(8,128)(2,1)} fusion(bf16[3,1024,512]{2,1,0:T(8,128)(2,1)} %param.14, bf16[512,1024]{1,0:T(8,128)(2,1)S(1)} %copy-done.17), kind=kOutput, calls=%fused_computation.129 | convolution fusion | flops 542375936 | bytes 2621440 | tf_op jit(solution)/shard_map/dot_general | solution.py:17
  71.8 0.0 collective-permute-done.3
  71.8 3.8 %collective-permute-start.9 = (bf16[512,512]{1,0:T(8,128)(2,1)}, bf16[512,512]{1,0:T(8,128)(2,1)}, u32[]{:S(2)}, u32[]{:S(2)}) collective-permute-start(bf16[512,512]{1,0:T(8,128)(2,1)} %convolution_convert_fusion), channel_id=1, source_target_pairs={{0,6},{1,7},{2,0},{3,1},{4,2},{5,3},{6,4},{7,5},{8,14},{9,15},{10,... | collective-permute-start | bytes 1572872 | tf_op jit(solution)/shard_map/ppermute | solution.py:9
  75.6 0.0 collective-permute-done.4
  75.6 0.0 copy-done.8
  75.6 0.8 copy-done.9
  76.4 0.0 collective-permute-start.1
  76.4 0.0 copy-done.11
  76.5 3.9 %fusion.47 = bf16[512,1024]{1,0:T(8,128)(2,1)S(1)} fusion(bf16[512,1024]{1,0:T(8,128)(2,1)} %fusion.15, bf16[512,1024]{1,0:T(8,128)(2,1)S(1)} %copy-done.7, f32[1024]{0:T(1024)S(1)} %copy-done.11, bf16[512,512]{1,0:T(8,128)(2,1)} %copy-done.9, bf16[512,512]{1,0:T(8,128)(2,1)} %copy-done.8, bf16[3,1024,512]{2,1,0:T(8,128)(2,1)} %param.14, f32[512]{0:T(512)S(1)} %copy-done.13), kind=kOutput, calls=%fused_computation.88 | convolution fusion | flops 1084751872 | bytes 6297600 | tf_op jit(solution)/shard_map/dot_general | solution.py:26
  80.4 0.0 collective-permute-done.5
  80.4 4.1 %collective-permute-start.2 = (bf16[512,512]{1,0:T(8,128)(2,1)}, bf16[512,512]{1,0:T(8,128)(2,1)}, u32[]{:S(2)}, u32[]{:S(2)}) collective-permute-start(bf16[512,512]{1,0:T(8,128)(2,1)} %convolution_convert_fusion.7), channel_id=1, source_target_pairs={{0,6},{1,7},{2,0},{3,1},{4,2},{5,3},{6,4},{7,5},{8,14},{9,15},{10,... | collective-permute-start | bytes 1572872 | tf_op jit(solution)/shard_map/ppermute | solution.py:9
  84.5 0.0 collective-permute-done.6
  84.5 4.2 %fusion.55 = bf16[512,1024]{1,0:T(8,128)(2,1)S(1)} fusion(bf16[512,1024]{1,0:T(8,128)(2,1)} %fusion.39, bf16[512,1024]{1,0:T(8,128)(2,1)} %param.16, f32[1024]{0:T(1024)S(1)} %copy-done.11, bf16[512,512]{1,0:T(8,128)(2,1)} %collective-permute-done.6, bf16[512,512]{1,0:T(8,128)(2,1)} %collective-permute-done.5, bf16[3,1024,512]{2,1,0:T(8,128)(2,1)} %param.14, ...), kind=kOutput, calls=%fused_computation.96 | convolution fusion | flops 1084751872 | bytes 6297600 | tf_op jit(solution)/shard_map/dot_general | solution.py:26
  88.7 0.0 collective-permute-done.8
  88.7 6.0 %collective-permute-done.9 = bf16[512,512]{1,0:T(8,128)(2,1)} collective-permute-done((bf16[512,512]{1,0:T(8,128)(2,1)}, bf16[512,512]{1,0:T(8,128)(2,1)}, u32[]{:S(2)}, u32[]{:S(2)}) %collective-permute-start.9) | collective-permute-done | bytes 524320 | tf_op jit(solution)/shard_map/ppermute | solution.py:9
  94.7 5.2 %fusion.63 = bf16[512,1024]{1,0:T(8,128)(2,1)} fusion(bf16[512,1024]{1,0:T(8,128)(2,1)} %fusion.23, bf16[512,1024]{1,0:T(8,128)(2,1)} %param.16, f32[1024]{0:T(1024)S(1)} %copy-done.11, bf16[512,512]{1,0:T(8,128)(2,1)} %collective-permute-done.9, bf16[512,512]{1,0:T(8,128)(2,1)} %collective-permute-done.8, bf16[3,1024,512]{2,1,0:T(8,128)(2,1)} %param.14, ...), kind=kOutput, calls=%fused_computation.104 | convolution fusion | flops 1084751872 | bytes 6297600 | tf_op jit(solution)/shard_map/dot_general | solution.py:26
  100.0 5.9 %collective-permute-done.1 = bf16[512,512]{1,0:T(8,128)(2,1)} collective-permute-done((bf16[512,512]{1,0:T(8,128)(2,1)}, bf16[512,512]{1,0:T(8,128)(2,1)}, u32[]{:S(2)}, u32[]{:S(2)}) %collective-permute-start.1) | collective-permute-done | bytes 524320 | tf_op jit(solution)/shard_map/ppermute | solution.py:9
  105.8 9.8 %collective-permute-done.2 = bf16[512,512]{1,0:T(8,128)(2,1)} collective-permute-done((bf16[512,512]{1,0:T(8,128)(2,1)}, bf16[512,512]{1,0:T(8,128)(2,1)}, u32[]{:S(2)}, u32[]{:S(2)}) %collective-permute-start.2) | collective-permute-done | bytes 524320 | tf_op jit(solution)/shard_map/ppermute | solution.py:9
  115.6 5.2 %fusion.31 = bf16[512,1024]{1,0:T(8,128)(2,1)} fusion(bf16[512,1024]{1,0:T(8,128)(2,1)} %fusion.7, bf16[512,1024]{1,0:T(8,128)(2,1)} %param.16, f32[1024]{0:T(1024)S(1)} %copy-done.11, bf16[512,512]{1,0:T(8,128)(2,1)} %collective-permute-done.2, bf16[512,512]{1,0:T(8,128)(2,1)} %collective-permute-done.1, bf16[3,1024,512]{2,1,0:T(8,128)(2,1)} %param.14, ...), kind=kOutput, calls=%fused_computation.72 | convolution fusion | flops 1084751872 | bytes 6297600 | tf_op jit(solution)/shard_map/dot_general | solution.py:26
  120.8 3.4 %pad_maximum_fusion = bf16[2048,1024]{1,0:T(8,128)(2,1)} fusion(bf16[512,1024]{1,0:T(8,128)(2,1)} %fusion.63, bf16[512,1024]{1,0:T(8,128)(2,1)S(1)} %fusion.55, bf16[512,1024]{1,0:T(8,128)(2,1)S(1)} %fusion.47, bf16[512,1024]{1,0:T(8,128)(2,1)} %fusion.31), kind=kLoop, calls=%fused_computation | loop fusion | flops 16777216 | bytes 8388608 | tf_op jit(solution)/shard_map/concatenate | solution.py:78
  (17 shorter events, 0.0 us)
Async XLA Ops:
  0.0 13.3 %copy-start = (bf16[512,1024]{1,0:T(8,128)(2,1)S(1)}, bf16[512,1024]{1,0:T(8,128)(2,1)}, u32[]{:S(2)}) copy-start(bf16[512,1024]{1,0:T(8,128)(2,1)} %param.12) | copy-start | bytes 3145732
  0.0 5.6 %copy-start.4 = (bf16[3,1024,512]{2,1,0:T(8,128)(2,1)S(1)}, bf16[3,1024,512]{2,1,0:T(8,128)(2,1)}, u32[]{:S(2)}) copy-start(bf16[3,1024,512]{2,1,0:T(8,128)(2,1)} %param.10) | copy-start | bytes 9437188
  0.0 5.6 %copy-start.1 = (bf16[2048,1024]{1,0:T(8,128)(2,1)S(1)}, bf16[2048,1024]{1,0:T(8,128)(2,1)}, u32[]{:S(2)}) copy-start(bf16[2048,1024]{1,0:T(8,128)(2,1)} %param.9) | copy-start | bytes 12582916
  2.6 58.1 %collective-permute-start = (bf16[512,512]{1,0:T(8,128)(2,1)S(1)}, bf16[512,512]{1,0:T(8,128)(2,1)S(1)}, u32[]{:S(2)}, u32[]{:S(2)}) collective-permute-start(bf16[512,512]{1,0:T(8,128)(2,1)S(1)} %convolution_convert_fusion.9), channel_id=1, source_target_pairs={{0,1},{1,2},{2,3},{3,4},{4,5},{5,6},{6,7},{7,0},{8,9},{9,10},{10,1... | collective-permute-start | bytes 1572872 | tf_op jit(solution)/shard_map/ppermute | solution.py:9
  7.3 38.9 %collective-permute-start.7 = (bf16[512,512]{1,0:T(8,128)(2,1)}, bf16[512,512]{1,0:T(8,128)(2,1)}, u32[]{:S(2)}, u32[]{:S(2)}) collective-permute-start(bf16[512,512]{1,0:T(8,128)(2,1)} %convolution_convert_fusion.2), channel_id=1, source_target_pairs={{0,7},{1,0},{2,1},{3,2},{4,3},{5,4},{6,5},{7,6},{8,15},{9,8},{10,9... | collective-permute-start | bytes 1572872 | tf_op jit(solution)/shard_map/ppermute | solution.py:9
  12.4 0.9 copy-start.10
  12.4 0.9 copy-start.12
  17.9 3.4 %copy-start.15 = (bf16[512,1024]{1,0:T(8,128)(2,1)S(1)}, bf16[512,1024]{1,0:T(8,128)(2,1)}, u32[]{:S(2)}) copy-start(bf16[512,1024]{1,0:T(8,128)(2,1)} %fusion.15) | copy-start | bytes 3145732
  21.3 6.8 %copy-start.2 = (bf16[2048,1024]{1,0:T(8,128)(2,1)S(1)}, bf16[2048,1024]{1,0:T(8,128)(2,1)}, u32[]{:S(2)}) copy-start(bf16[2048,1024]{1,0:T(8,128)(2,1)} %param.9) | copy-start | bytes 12582916
  21.3 6.8 %copy-start.5 = (bf16[3,1024,512]{2,1,0:T(8,128)(2,1)S(1)}, bf16[3,1024,512]{2,1,0:T(8,128)(2,1)}, u32[]{:S(2)}) copy-start(bf16[3,1024,512]{2,1,0:T(8,128)(2,1)} %param.10) | copy-start | bytes 9437188
  21.3 50.5 %collective-permute-start.3 = (bf16[512,512]{1,0:T(8,128)(2,1)}, bf16[512,512]{1,0:T(8,128)(2,1)S(1)}, u32[]{:S(2)}, u32[]{:S(2)}) collective-permute-start(bf16[512,512]{1,0:T(8,128)(2,1)} %convolution_convert_fusion.6), channel_id=1, source_target_pairs={{0,2},{1,3},{2,4},{3,5},{4,6},{5,7},{6,0},{7,1},{8,10},{9,11},{10,... | collective-permute-start | bytes 1572872 | tf_op jit(solution)/shard_map/ppermute | solution.py:9
  24.4 51.2 %collective-permute-start.4 = (bf16[512,512]{1,0:T(8,128)(2,1)}, bf16[512,512]{1,0:T(8,128)(2,1)S(1)}, u32[]{:S(2)}, u32[]{:S(2)}) collective-permute-start(bf16[512,512]{1,0:T(8,128)(2,1)} %convolution_convert_fusion.5), channel_id=1, source_target_pairs={{0,6},{1,7},{2,0},{3,1},{4,2},{5,3},{6,4},{7,5},{8,14},{9,15},{10,... | collective-permute-start | bytes 1572872 | tf_op jit(solution)/shard_map/ppermute | solution.py:9
  35.6 3.4 %copy-start.3 = (bf16[2048,1024]{1,0:T(8,128)(2,1)S(1)}, bf16[2048,1024]{1,0:T(8,128)(2,1)}, u32[]{:S(2)}) copy-start(bf16[2048,1024]{1,0:T(8,128)(2,1)} %param.9) | copy-start | bytes 12582916
  35.6 4.0 %copy-start.6 = (bf16[3,1024,512]{2,1,0:T(8,128)(2,1)S(1)}, bf16[3,1024,512]{2,1,0:T(8,128)(2,1)}, u32[]{:S(2)}) copy-start(bf16[3,1024,512]{2,1,0:T(8,128)(2,1)} %param.10) | copy-start | bytes 9437188
  39.0 2.4 %copy-start.14 = (bf16[512,1024]{1,0:T(8,128)(2,1)S(1)}, bf16[512,1024]{1,0:T(8,128)(2,1)}, u32[]{:S(2)}) copy-start(bf16[512,1024]{1,0:T(8,128)(2,1)} %fusion.39) | copy-start | bytes 3145732
  39.0 41.4 %collective-permute-start.5 = (bf16[512,512]{1,0:T(8,128)(2,1)}, bf16[512,512]{1,0:T(8,128)(2,1)}, u32[]{:S(2)}, u32[]{:S(2)}) collective-permute-start(bf16[512,512]{1,0:T(8,128)(2,1)} %convolution_convert_fusion.4), channel_id=1, source_target_pairs={{0,2},{1,3},{2,4},{3,5},{4,6},{5,7},{6,0},{7,1},{8,10},{9,11},{10,... | collective-permute-start | bytes 1572872 | tf_op jit(solution)/shard_map/ppermute | solution.py:9
  46.2 38.3 %collective-permute-start.6 = (bf16[512,512]{1,0:T(8,128)(2,1)}, bf16[512,512]{1,0:T(8,128)(2,1)}, u32[]{:S(2)}, u32[]{:S(2)}) collective-permute-start(bf16[512,512]{1,0:T(8,128)(2,1)} %convolution_convert_fusion.3), channel_id=1, source_target_pairs={{0,6},{1,7},{2,0},{3,1},{4,2},{5,3},{6,4},{7,5},{8,14},{9,15},{10,... | collective-permute-start | bytes 1572872 | tf_op jit(solution)/shard_map/ppermute | solution.py:9
  54.4 3.3 %copy-start.16 = (bf16[512,1024]{1,0:T(8,128)(2,1)S(1)}, bf16[512,1024]{1,0:T(8,128)(2,1)}, u32[]{:S(2)}) copy-start(bf16[512,1024]{1,0:T(8,128)(2,1)} %fusion.23) | copy-start | bytes 3145732
  60.6 28.1 %collective-permute-start.8 = (bf16[512,512]{1,0:T(8,128)(2,1)}, bf16[512,512]{1,0:T(8,128)(2,1)}, u32[]{:S(2)}, u32[]{:S(2)}) collective-permute-start(bf16[512,512]{1,0:T(8,128)(2,1)} %convolution_convert_fusion.1), channel_id=1, source_target_pairs={{0,2},{1,3},{2,4},{3,5},{4,6},{5,7},{6,0},{7,1},{8,10},{9,11},{10,... | collective-permute-start | bytes 1572872 | tf_op jit(solution)/shard_map/ppermute | solution.py:9
  65.5 3.3 %copy-start.17 = (bf16[512,1024]{1,0:T(8,128)(2,1)S(1)}, bf16[512,1024]{1,0:T(8,128)(2,1)}, u32[]{:S(2)}) copy-start(bf16[512,1024]{1,0:T(8,128)(2,1)} %fusion.7) | copy-start | bytes 3145732
  68.8 7.6 %copy-start.7 = (bf16[512,1024]{1,0:T(8,128)(2,1)S(1)}, bf16[512,1024]{1,0:T(8,128)(2,1)}, u32[]{:S(2)}) copy-start(bf16[512,1024]{1,0:T(8,128)(2,1)} %param.16) | copy-start | bytes 3145732
  68.8 7.6 %copy-start.11 = (f32[1024]{0:T(1024)S(1)}, f32[1024]{0:T(1024)}, u32[]{:S(2)}) copy-start(f32[1024]{0:T(1024)} %param.17) | copy-start | bytes 12292
  68.8 7.6 %copy-start.13 = (f32[512]{0:T(512)S(1)}, f32[512]{0:T(512)}, u32[]{:S(2)}) copy-start(f32[512]{0:T(512)} %param.15) | copy-start | bytes 6148
  71.8 3.8 %copy-start.8 = (bf16[512,512]{1,0:T(8,128)(2,1)}, bf16[512,512]{1,0:T(8,128)(2,1)S(1)}, u32[]{:S(2)}) copy-start(bf16[512,512]{1,0:T(8,128)(2,1)S(1)} %collective-permute-done.3) | copy-start | bytes 1572868
  71.8 22.9 %collective-permute-start.9 = (bf16[512,512]{1,0:T(8,128)(2,1)}, bf16[512,512]{1,0:T(8,128)(2,1)}, u32[]{:S(2)}, u32[]{:S(2)}) collective-permute-start(bf16[512,512]{1,0:T(8,128)(2,1)} %convolution_convert_fusion), channel_id=1, source_target_pairs={{0,6},{1,7},{2,0},{3,1},{4,2},{5,3},{6,4},{7,5},{8,14},{9,15},{10,... | collective-permute-start | bytes 1572872 | tf_op jit(solution)/shard_map/ppermute | solution.py:9
  75.6 0.8 copy-start.9
  76.4 29.4 %collective-permute-start.1 = (bf16[512,512]{1,0:T(8,128)(2,1)}, bf16[512,512]{1,0:T(8,128)(2,1)}, u32[]{:S(2)}, u32[]{:S(2)}) collective-permute-start(bf16[512,512]{1,0:T(8,128)(2,1)} %convolution_convert_fusion.8), channel_id=1, source_target_pairs={{0,2},{1,3},{2,4},{3,5},{4,6},{5,7},{6,0},{7,1},{8,10},{9,11},{10,... | collective-permute-start | bytes 1572872 | tf_op jit(solution)/shard_map/ppermute | solution.py:9
  80.4 35.2 %collective-permute-start.2 = (bf16[512,512]{1,0:T(8,128)(2,1)}, bf16[512,512]{1,0:T(8,128)(2,1)}, u32[]{:S(2)}, u32[]{:S(2)}) collective-permute-start(bf16[512,512]{1,0:T(8,128)(2,1)} %convolution_convert_fusion.7), channel_id=1, source_target_pairs={{0,6},{1,7},{2,0},{3,1},{4,2},{5,3},{6,4},{7,5},{8,14},{9,15},{10,... | collective-permute-start | bytes 1572872 | tf_op jit(solution)/shard_map/ppermute | solution.py:9

commit v2 on v1

v2 whole, which is shorter than its diff:
```python
import functools

import jax
import jax.numpy as jnp
from jax import lax
from jax.experimental import pallas as pl
from jax.experimental.pallas import tpu as pltpu
from jax.sharding import PartitionSpec as P

MESH = pl.DeviceIdType.MESH
BF16 = jnp.bfloat16
F32 = jnp.float32


def gelu(v):
    return 0.5 * v * (1.0 + jnp.tanh(0.7978845608028654 * (v + 0.044715 * (v * v * v))))


def dot(a, b):
    return jnp.dot(a, b, preferred_element_type=F32)


def kernel(
    size, x_hbm, t1_hbm, b1, w1_hbm, pb1, t2_hbm, b2, w2_hbm, pb2, out_hbm,
    xv, t1, w1, t2, w2, act, halo_out, halo_in, far_out, far_in, centre,
    x_sem, t1_sem, t2_sem, w_sem, halo_send, halo_recv, far_send, far_recv, out_sem,
):
    rows = xv.shape[0]
    step = rows // 8
    d = rows // 4
    me = lax.axis_index("seq")
    fwd = [lax.rem(me + k, size) for k in (1, 2)]
    back = [lax.rem(me + size - k, size) for k in (1, 2)]

    barrier = pltpu.get_barrier_semaphore()
    for other in fwd + back:
        pl.semaphore_signal(barrier, inc=1, device_id={"seq": other}, device_id_type=MESH)

    def part(c):
        return pl.ds(pl.multiple_of(c * step, step), step)

    def load_x(c):
        return pltpu.make_async_copy(x_hbm.at[part(c)], xv.at[part(c)], x_sem.at[c])

    def load_tap(k, hbm, vmem, sem):
        return pltpu.make_async_copy(hbm.at[k], vmem.at[k], sem.at[k])

    load_w1 = pltpu.make_async_copy(w1_hbm, w1, w_sem.at[0])
    load_w2 = pltpu.make_async_copy(w2_hbm, w2, w_sem.at[1])
    load_x(0).start()
    load_tap(2, t1_hbm, t1, t1_sem).start()
    load_x(1).start()
    load_x(6).start()
    load_tap(0, t1_hbm, t1, t1_sem).start()
    load_x(7).start()
    load_x(2).start()
    load_x(4).start()
    load_tap(1, t1_hbm, t1, t1_sem).start()
    load_w1.start()
    for k in range(3):
        load_tap(k, t2_hbm, t2, t2_sem).start()
    load_x(3).start()
    load_x(5).start()
    load_w2.start()

    def halo_copy(m, j):
        return pltpu.make_async_remote_copy(
            src_ref=halo_out.at[m, j], dst_ref=halo_in.at[m, j],
            send_sem=halo_send.at[m, j], recv_sem=halo_recv.at[m, j],
            device_id={"seq": fwd[0] if m == 0 else back[0]}, device_id_type=MESH,
        )

    def far_copy(m, c):
        return pltpu.make_async_remote_copy(
            src_ref=far_out.at[m, c], dst_ref=far_in.at[m, c],
            send_sem=far_send.at[m, c], recv_sem=far_recv.at[m, c],
            device_id={"seq": fwd[1] if m == 0 else back[1]}, device_id_type=MESH,
        )

    def activate(c):
        load_x(c).wait()
        act[part(c)] = gelu(xv[part(c)].astype(F32)).astype(BF16)

    activate(0)
    load_tap(2, t1_hbm, t1, t1_sem).wait()
    pl.semaphore_wait(barrier, 4)
    for m in (1, 0):
        tap = 2 * m
        first = 0 if m == 1 else 6
        if m == 0:
            load_tap(tap, t1_hbm, t1, t1_sem).wait()

        @pl.loop(0, 2)
        def _(j):
            if m == 0:
                activate(first + j)
            else:
                @pl.when(j == 1)
                def _():
                    activate(first + j)
            halo_out[m, j] = dot(act[part(first + j)], t1[tap]).astype(BF16)
            halo_copy(m, j).start()

    def layer(c, total):
        middle = gelu(total + b1[...]).astype(BF16)
        one = (xv[part(c)].astype(F32) + dot(middle, w1[...]) + pb1[...]).astype(BF16)
        xv[part(c)] = one
        far_act = gelu(one.astype(F32)).astype(BF16)
        far_out[0, c] = dot(far_act, t2[0]).astype(BF16)
        far_copy(0, c).start()
        far_out[1, c] = dot(far_act, t2[2]).astype(BF16)
        far_copy(1, c).start()
        centre[part(c)] = dot(far_act, t2[1])

    activate(2)
    activate(4)
    load_tap(1, t1_hbm, t1, t1_sem).wait()
    load_w1.wait()
    for k in range(3):
        load_tap(k, t2_hbm, t2, t2_sem).wait()

    @pl.loop(0, 4)
    def _(i):
        j, m = i // 2, lax.rem(i, 2)
        c = 2 + j + 2 * m
        layer(c, dot(act[part(c - 2)], t1[0]) + dot(act[part(c)], t1[1]) + dot(act[part(c + 2)], t1[2]))

        @pl.when(i == 1)
        def _():
            activate(3)
            activate(5)

    @pl.loop(0, 4)
    def _(i):
        j, m = i // 2, lax.rem(i, 2)
        c = 6 * m + j
        near = dot(act[part(c)], t1[1]) + dot(act[part(c + 2 - 4 * m)], t1[2 - 2 * m])

        @pl.when(m == 0)
        def _():
            halo_copy(0, j).wait_recv()

        @pl.when(m == 1)
        def _():
            halo_copy(1, j).wait_recv()

        layer(c, near + halo_in[m, j].astype(F32))

    load_w2.wait()

    def finish(c):
        far_copy(0, c).wait_recv()
        far_copy(1, c).wait_recv()
        total = centre[part(c)] + far_in[0, c].astype(F32) + far_in[1, c].astype(F32)
        middle = gelu(total + b2[...]).astype(BF16)
        xv[part(c)] = (xv[part(c)].astype(F32) + dot(middle, w2[...]) + pb2[...]).astype(BF16)
        pltpu.make_async_copy(xv.at[part(c)], out_hbm.at[part(c)], out_sem.at[c]).start()

    @pl.loop(0, 8)
    def _(i):
        edge = i // 4
        k = lax.rem(i, 4)
        j, m = k // 2, lax.rem(k, 2)
        finish(j + (1 - edge) * (2 + 2 * m) + edge * 6 * m)

    for m in range(2):
        for j in range(2):
            halo_copy(m, j).wait_send()

    @pl.loop(0, 8)
    def _(c):
        far_copy(0, c).wait_send()
        far_copy(1, c).wait_send()
        pltpu.make_async_copy(xv.at[part(c)], out_hbm.at[part(c)], out_sem.at[c]).wait()


def per_device(x, t1, b1, w1, pb1, t2, b2, w2, pb2):
    rows, wide = x.shape
    mid = w1.shape[0]
    step = rows // 8
    hbm = pl.BlockSpec(memory_space=pl.ANY)
    vmem = pl.BlockSpec(memory_space=pltpu.VMEM)
    dma = pltpu.SemaphoreType.DMA
    flops = 2 * rows * wide * mid * 8
    return pl.pallas_call(
        functools.partial(kernel, lax.axis_size("seq")),
        out_shape=jax.ShapeDtypeStruct((rows, wide), BF16),
        in_specs=[hbm, hbm, vmem, hbm, vmem, hbm, vmem, hbm, vmem],
        out_specs=hbm,
        scratch_shapes=[
            pltpu.VMEM((rows, wide), BF16),
            pltpu.VMEM((3, wide, mid), BF16),
            pltpu.VMEM((mid, wide), BF16),
            pltpu.VMEM((3, wide, mid), BF16),
            pltpu.VMEM((mid, wide), BF16),
            pltpu.VMEM((rows, wide), BF16),
            pltpu.VMEM((2, 2, step, mid), BF16),
            pltpu.VMEM((2, 2, step, mid), BF16),
            pltpu.VMEM((2, 8, step, mid), BF16),
            pltpu.VMEM((2, 8, step, mid), BF16),
            pltpu.VMEM((rows, mid), F32),
            dma((8,)), dma((3,)), dma((3,)), dma((2,)),
            dma((2, 2)), dma((2, 2)), dma((2, 8)), dma((2, 8)), dma((8,)),
        ],
        compiler_params=pltpu.CompilerParams(
            collective_id=0, has_side_effects=True, vmem_limit_bytes=56 * 2**20
        ),
        cost_estimate=pl.CostEstimate(flops=flops, bytes_accessed=16 * 2**20, transcendentals=0),
    )(x, t1, b1.reshape(1, mid), w1, pb1.reshape(1, wide), t2, b2.reshape(1, mid), w2, pb2.reshape(1, wide))


def solution(mesh):
    return jax.shard_map(
        per_device,
        mesh=mesh,
        in_specs=(P(("grp", "seq"), None), P(), P(), P(), P(), P(), P(), P(), P()),
        out_specs=P(("grp", "seq"), None),
        check_vma=False,
    )
```

time: 124 us -> 117 us (0.944); the launches traced: 124 us -> 115 us
  Pallas kernels: 0 us -> 110 us
  matrix products: 75.4 us -> 0 us
  starting transfers between devices: 22.1 us -> 0 us
  waiting for transfers between devices: 21.7 us -> 0 us
  other arithmetic: 3.4 us -> 0 us
  local copies, waits for them, and re-layouts: 1.45 us -> 4.64 us
    pallas_call x0 -> x1, Pallas kernels: none -> 110 us  [per_device(): pl.pallas_call(functools.partial(kernel, lax.axis_size('seq')), out_shape...]
    dot_general x24 -> x0, matrix products: 75.4 us -> none  [the longest x8 37.7 us: finish(): branch = jnp.dot(middle, point, preferred_element_type=jnp.float32)]
    ppermute x10 -> x0, starting transfers between devices: 22.1 us -> none  [shifted(): lax.ppermute(value, axis, [(i, (i + by) % size) for i in range(size)])]
    ppermute x10 -> x0, waiting for transfers between devices: 21.7 us -> none  [shifted(): lax.ppermute(value, axis, [(i, (i + by) % size) for i in range(size)])]
    concatenate x1 -> x0, other arithmetic: 3.4 us -> none  [per_device(): return jnp.concatenate(outs, axis=0)]
    unnamed x36 -> x1, local copies, waits for them, and re-layouts: 1.45 us -> 4.64 us
  transfers between devices with their start and end apart: 10 -> 0, of which waited for: 3 -> 0; matrix products, arithmetic and copies ran while one was open for 55% -> 0% of each run, Pallas kernels for 0% -> 0%
where the time goes in v2:
time: 117 us; the launch traced here: 115 us
  Pallas kernels  110 us (94%)
  local copies, waits for them, and re-layouts  4.64 us (4%)
    pallas_call x1, Pallas kernels, per_device(): pl.pallas_call(functools.partial(kernel, lax.axis_size('seq')), out_shape...  110 us
    unnamed x1, local copies, waits for them, and re-layouts  4.64 us

profile of v2, /device:TPU:0, one launch (start us, length us, event | category | flops | bytes accessed | tf_op | source)
XLA Modules:
  0.0 114.7 jit_solution(18009757312076737240)
XLA Ops:
  0.0 110.0 %shard_map.91 = bf16[2048,1024]{1,0:T(8,128)(2,1)} custom-call(bf16[2048,1024]{1,0:T(8,128)(2,1)} %x_hbm.1, bf16[3,1024,512]{2,1,0:T(8,128)(2,1)} %t1_hbm.1, f32[1,512]{1,0:T(1,128)} %bitcast.6, bf16[512,1024]{1,0:T(8,128)(2,1)} %w1_hbm.1, f32[1,1024]{1,0:T(1,128)} %bitcast.4, bf16[3,1024,512]{2,1,0:T(8,128)(2,1)} %t2_hbm.1, f32[1,512]{1,0:T(1,128)} %bitcast.7, ...), custom_call_target="tpu_custom_call" | custom-call | flops 17179869184 | bytes 16777216 | tf_op jit(solution)/shard_map/pallas_call | solution.py:185
  110.0 4.6 %copy.11 = bf16[2048,1024]{1,0:T(8,128)(2,1)} copy(bf16[2048,1024]{1,0:T(8,128)(2,1)} %shard_map.91) | data formatting | bytes 8388608
